TPU v7x, 32 devices: a whole 2x2x4 slice. The times are simulated.
32 devices in a mesh: pair: 8 (over z, core), virt: 4 (over y, x).
Axes of the slice: x: 2, y: 2, z: 4, core: 2. Of those that a mesh axis runs over, the one named last changes fastest.
Arguments:
- amplitudes: float32 [16, 1024, 4096], P('virt', 'pair'), may hold values from -0.9 to 0.9
- integrals: float32 [16, 384, 4096], P('virt', 'pair'), may hold values from -0.09375 to 0.09375
- tile_flags: int32 [16], P('virt'), may hold values 0 or 1
- live_count: int32 [4], replicated, may hold values from 1 to 4, as said below
- pair_occ: int32 [1024, 2], P(('pair', 'virt')), may hold values from 0 to 199
- occ_energy: float32 [200], replicated, may hold values from -2.5 to -0.3
- ab_energy: float32 [384], replicated, may hold values from 0.6 to 3
Outputs:
- ladder: float32 [1024, 384], P(('pair', 'virt'))
- update: float32 [1024, 384], P(('pair', 'virt'))
Inputs may be any that keep to these rules, and one draw needn't show every extreme that they name: `live_count`: entry v is how many of the 4 slots of virt index v hold tile pairs: its slots below that number do, and the contents of the others are not to be used. At some index it is 4, and at the index half the axis away it is 1.
All inputs are finite; a program needn't handle non-finite values. No bound on the sum of `tile_flags` on one device may be relied on, other than what follows from the above.
Results may differ from a plain program's by a relative error of at most 0.0001.
Values sent between devices are 32-bit elements; how exact they have to be, the bound alone decides.
A program may use at most 128 MiB of HBM per device.

v0:
```python
import jax
import jax.numpy as jnp
from jax import lax
from jax.sharding import PartitionSpec as P

TILE = 64


def symmetric(integrals, tile_flags):
    shaped = integrals.reshape(integrals.shape[0], integrals.shape[1], TILE, TILE)
    swapped = jnp.swapaxes(shaped, 2, 3).reshape(integrals.shape)
    return integrals + tile_flags.astype(jnp.float32)[:, None, None] * swapped


def tile_product(amp_tile, int_rows):
    return lax.dot_general(
        amp_tile,
        int_rows,
        (((1,), (1,)), ((), ())),
        precision=lax.Precision.HIGHEST,
        preferred_element_type=jnp.float32,
    )


def take_slot(stack, slot_at):
    return lax.dynamic_index_in_dim(stack, slot_at, 0, keepdims=False)


def contract(amp_stack, int_stack, first_slot, last_slot, pair_rows):
    piece_rows = lax.all_gather(int_stack, "pair", axis=1, tiled=True)

    def add_tile(slot_at, running):
        return running + tile_product(take_slot(amp_stack, slot_at), take_slot(piece_rows, slot_at))

    return lax.fori_loop(
        first_slot, last_slot, add_tile, jnp.zeros((pair_rows, piece_rows.shape[1]), jnp.float32)
    )


def on_device(amplitudes, integrals, tile_flags, live_count, pair_occ, occ_energy, ab_energy):
    pair_rows = amplitudes.shape[1]
    virt_index = lax.axis_index("virt")
    own_count = live_count[virt_index]
    sym_integrals = symmetric(integrals, tile_flags)
    partial_value = contract(amplitudes, sym_integrals, 0, own_count, pair_rows)
    ladder = lax.psum_scatter(partial_value, "virt", scatter_dimension=0, tiled=True)
    occ_range = jnp.arange(occ_energy.shape[0], dtype=jnp.int32)
    first_energy = jnp.sum(
        jnp.where(pair_occ[:, 0:1] == occ_range[None, :], occ_energy[None, :], 0.0), axis=1
    )
    second_energy = jnp.sum(
        jnp.where(pair_occ[:, 1:2] == occ_range[None, :], occ_energy[None, :], 0.0), axis=1
    )
    denominator = ab_energy[None, :] - first_energy[:, None] - second_energy[:, None]
    return (ladder, ladder / denominator)


def solution(mesh):
    return jax.shard_map(
        on_device,
        mesh=mesh,
        in_specs=(
            P("virt", "pair", None),
            P("virt", "pair", None),
            P("virt"),
            P(),
            P(("pair", "virt"), None),
            P(),
            P(),
        ),
        out_specs=(P(("pair", "virt"), None), P(("pair", "virt"), None)),
        check_vma=False,
    )
```

profile of v0, /device:TPU:0, one launch (start us, length us, event | category | flops | bytes accessed | tf_op | source)
XLA Modules:
  0.0 324.2 jit_solution(11953718747821690618)
XLA Ops:
  7.2 0.0 all-gather.2.cloned.1.call-start
  7.2 6.1 %reshape.15 = f32[4,48,64,64]{3,2,1,0:T(8,128)} reshape(f32[4,48,4096]{2,1,0:T(8,128)} %param.10) | data formatting | bytes 6291456 | tf_op jit(solution)/shard_map/reshape | solution.py:10
  13.3 6.6 %copy.10 = f32[4,48,64,64]{2,3,1,0:T(8,128)} copy(f32[4,48,64,64]{3,2,1,0:T(8,128)} %reshape.15) | data formatting | bytes 6291456 | tf_op jit(solution)/shard_map/reshape | solution.py:10
  19.9 0.0 copy-start.5
  19.9 0.0 copy-start
  19.9 6.0 %reshape.16 = f32[4,48,4096]{2,1,0:T(8,128)} reshape(f32[4,48,64,64]{3,2,1,0:T(8,128)} %bitcast.22) | data formatting | bytes 6291456 | tf_op jit(solution)/shard_map/reshape | solution.py:11
  25.9 0.0 copy-done.5
  25.9 0.0 copy-done
  25.9 0.0 copy-start.6
  25.9 4.1 %multiply_add_fusion = f32[4,48,4096]{2,1,0:T(8,128)} fusion(f32[4,48,4096]{2,1,0:T(8,128)S(1)} %copy-done, f32[4,48,4096]{2,1,0:T(8,128)} %reshape.16, f32[4]{0:T(128)S(1)} %convert_element_type.3), kind=kLoop, calls=%fused_computation.7 | loop fusion | flops 1572864 | bytes 9437200 | tf_op jit(solution)/shard_map/add | solution.py:12
  30.1 0.0 all-gather.2.cloned.1.call-update
  30.1 0.0 reduce-scatter.2.cloned.1.call-start
  30.1 0.0 copy-done.6
  30.1 0.6 dynamic_slice.11
  30.7 222.1 %all-gather.2.cloned.1.call-done = f32[4,384,4096]{2,1,0:T(8,128)} async-done(((f32[4,48,4096]{2,1,0:T(8,128)}), f32[4,384,4096]{2,1,0:T(8,128)}) %all-gather.2.cloned.1.call-update) | async-done | bytes 25165840 | tf_op jit(solution)/shard_map/all_gather | solution.py:30
  252.8 0.0 copy-start.4
  252.8 0.0 copy-start.3
  252.8 0.0 copy-start.2
  252.9 20.3 %while.10 = (s32[]{:T(128)}, f32[128,384]{1,0:T(8,128)S(1)}, s32[]{:T(128)}, f32[4,128,4096]{2,1,0:T(8,128)}, f32[4,384,4096]{2,1,0:T(8,128)}, /*index=5*/s32[]{:T(128)}, s32[]{:T(128)}, s32[]{:T(128)}) while((s32[]{:T(128)}, f32[128,384]{1,0:T(8,128)S(1)}, s32[]{:T(128)}, f32[4,128,4096]{2,1,0:T(8,128)}, f32[4,384,4096]{2,1,0:T(8,128)}, ...), condition=%wide.region_1.2_spmd, body=%wide.region_0.1_spmd.sunk | while | flops 2415968256 | bytes 8782967 | solution.py:35
  253.5 9.2 %fusion.16 = f32[128,384]{1,0:T(8,128)S(1)} fusion(f32[128,384]{1,0:T(8,128)S(1)} %get-tuple-element.86, f32[4,384,4096]{2,1,0:T(8,128)} %get-tuple-element.97, s32[]{:T(128)S(6)} %select_n.22, f32[4,128,4096]{2,1,0:T(8,128)} %get-tuple-element.96), kind=kOutput, calls=%fused_computation.5.clone.1 | convolution fusion | flops 2415968256 | bytes 8782848 | tf_op jit(solution)/shard_map/while/body/dot_general | solution.py:16
  263.4 9.2 %fusion.16 = f32[128,384]{1,0:T(8,128)S(1)} fusion(f32[128,384]{1,0:T(8,128)S(1)} %get-tuple-element.86, f32[4,384,4096]{2,1,0:T(8,128)} %get-tuple-element.97, s32[]{:T(128)S(6)} %select_n.22, f32[4,128,4096]{2,1,0:T(8,128)} %get-tuple-element.96), kind=kOutput, calls=%fused_computation.5.clone.1 | convolution fusion | flops 2415968256 | bytes 8782848 | tf_op jit(solution)/shard_map/while/body/dot_general | solution.py:16
  273.2 0.0 copy-start.1
  273.2 0.7 copy-done.1
  273.9 0.0 reduce-scatter.2.cloned.1.call-update
  273.9 0.0 copy-done.4
  273.9 0.0 copy-done.3
  273.9 0.2 select_reduce_fusion.1
  274.1 41.8 %reduce-scatter.2.cloned.1.call-done = f32[32,384]{1,0:T(8,128)} async-done(((f32[128,384]{1,0:T(8,128)}), f32[32,384]{1,0:T(8,128)}) %reduce-scatter.2.cloned.1.call-update) | async-done | bytes 49168 | tf_op jit(solution)/shard_map/reduce_scatter | solution.py:46
  315.9 0.0 copy-done.2
  315.9 1.5 subtract_divide_fusion
  (3 shorter events, 0.0 us)
Async XLA Ops:
  7.2 245.6 %all-gather.2.cloned.1.call-start = ((), (), s32[]{:S(2)}) async-start(), calls=%async_computation.1 | async-start | bytes 28311552 | tf_op jit(solution)/shard_map/all_gather | solution.py:30
  19.9 6.0 %copy-start.5 = (s32[4]{0:T(128)S(1)}, s32[4]{0:T(128)}, u32[]{:S(2)}) copy-start(s32[4]{0:T(128)} %param.11) | copy-start | bytes 52
  19.9 6.0 %copy-start = (f32[4,48,4096]{2,1,0:T(8,128)S(1)}, f32[4,48,4096]{2,1,0:T(8,128)}, u32[]{:S(2)}) copy-start(f32[4,48,4096]{2,1,0:T(8,128)} %param.10) | copy-start | bytes 9437188
  25.9 4.2 %copy-start.6 = (s32[4]{0:T(128)S(1)}, s32[4]{0:T(128)}, u32[]{:S(2)}) copy-start(s32[4]{0:T(128)} %param.12) | copy-start | bytes 52
  30.1 285.8 %reduce-scatter.2.cloned.1.call-start = ((), (), s32[]{:S(2)}) async-start(), calls=%async_computation.2 | async-start | bytes 245760 | tf_op jit(solution)/shard_map/reduce_scatter | solution.py:46
  252.8 21.1 %copy-start.4 = (s32[32,2]{0,1:T(2,128)S(1)}, s32[32,2]{0,1:T(2,128)}, u32[]{:S(2)}) copy-start(s32[32,2]{0,1:T(2,128)} %param.13) | copy-start | bytes 772
  252.8 21.1 %copy-start.3 = (f32[200]{0:T(256)S(1)}, f32[200]{0:T(256)}, u32[]{:S(2)}) copy-start(f32[200]{0:T(256)} %param.14) | copy-start | bytes 2404
  252.8 63.0 %copy-start.2 = (f32[384]{0:T(512)S(1)}, f32[384]{0:T(512)}, u32[]{:S(2)}) copy-start(f32[384]{0:T(512)} %param.15) | copy-start | bytes 4612
  273.2 0.7 copy-start.1
Sparse Core Ops, SparseCore 0:
  30.2 222.5 all-gather.1
  274.0 41.8 reduce-scatter.1
where the time goes:
time: 324 us
  waiting for transfers between devices  264 us (81%)
  local copies, waits for them, and re-layouts  20 us (6%)
  matrix products  18.3 us (6%)
  between operations  14.1 us (4%)
  other arithmetic  5.81 us (2%)
    all_gather x1, waiting for transfers between devices, contract(): piece_rows = lax.all_gather(int_stack, 'pair', axis=1, tiled=True)  222 us
    reduce_scatter x1, waiting for transfers between devices, on_device(): lax.psum_scatter(partial_value, 'virt', scatter_dimension=0, tiled=True)  41.8 us
    dot_general x2, matrix products, tile_product(): lax.dot_general(amp_tile, int_rows, (((1,), (1,)), ((), ())), precision=l...  18.3 us
    reshape x2, local copies, waits for them, and re-layouts, symmetric(): integrals.reshape(integrals.shape[0], integrals.shape[1], TILE, TILE)  12.7 us
  transfers between devices with their start and end apart: 2, of which 2 were waited for; matrix products, arithmetic and copies ran while one was open for 0% of the time, Pallas kernels for 0%

commit v1 on v0

v1 whole, which is shorter than its diff:
```python
import functools

import jax
import jax.numpy as jnp
from jax import lax
from jax.experimental import pallas as pl
from jax.experimental.pallas import tpu as pltpu
from jax.sharding import PartitionSpec as P

TILE = 64
CORES = 2
DEPTH = 512
MESH = pl.DeviceIdType.MESH


def symmetric(integrals, tile_flags):
    shaped = integrals.reshape(integrals.shape[0], integrals.shape[1], TILE, TILE)
    swapped = jnp.swapaxes(shaped, 2, 3).reshape(integrals.shape)
    return integrals + tile_flags.astype(jnp.float32)[:, None, None] * swapped


def split(x):
    high = x.astype(jnp.bfloat16)
    return high, (x - high.astype(jnp.float32)).astype(jnp.bfloat16)


def product(a, b):
    a_high, a_low = split(a)
    b_high, b_low = split(b)

    def dot(x, y):
        return lax.dot_general(x, y, (((1,), (1,)), ((), ())), preferred_element_type=jnp.float32)

    return dot(a_high, b_high) + (dot(a_high, b_low) + dot(a_low, b_high))


def kernel(queue, swaps, chips, n_virt, counts, a_ref, v_ref, out_ref, rows_all, a_out, a_in, v_out, v_in, acc, parts,
           xs, xr, zs, zr, cs, cr, rs, rr):
    pair = lax.axis_index("pair")
    virt = lax.axis_index("virt")
    z, core = pair // CORES, pair % CORES
    half = a_ref.shape[2] // 2
    slots = a_ref.shape[0]
    rows = v_ref.shape[1]
    pairs = a_ref.shape[1]
    out_rows = out_ref.shape[0]
    partner = lax.rem(virt + n_virt // 2, n_virt)
    live, keep, taken = counts[0], counts[1], counts[2]

    def chip_at(target):
        return (target * CORES + core, virt)

    twin = (z * CORES + 1 - core, virt)
    barrier = pltpu.get_barrier_semaphore()
    pl.semaphore_signal(barrier, inc=1, device_id=twin, device_id_type=MESH)
    for step in range(1, n_virt):
        pl.semaphore_signal(barrier, inc=1, device_id=(pair, lax.rem(virt + step, n_virt)), device_id_type=MESH)

    @pl.when(z > 0)
    def _():
        pl.semaphore_signal(barrier, inc=1, device_id=chip_at(z - 1), device_id_type=MESH)

    @pl.when(z < chips - 1)
    def _():
        pl.semaphore_signal(barrier, inc=1, device_id=chip_at(z + 1), device_id_type=MESH)

    greeted = n_virt + jnp.where(z > 0, 1, 0) + jnp.where(z < chips - 1, 1, 0)
    pl.semaphore_wait(barrier, greeted)

    def block(q, chip, core_at):
        start = pl.multiple_of((chip * CORES + core_at) * rows, 8)
        return rows_all.at[q, pl.ds(start, rows), :]

    def swap_a(j):
        return pltpu.make_async_remote_copy(
            src_ref=a_out.at[j], dst_ref=a_in.at[j], send_sem=xs.at[0, j], recv_sem=xr.at[0, j],
            device_id=(pair, partner), device_id_type=MESH)

    def swap_v(j):
        return pltpu.make_async_remote_copy(
            src_ref=v_out.at[j], dst_ref=v_in.at[j], send_sem=xs.at[1, j], recv_sem=xr.at[1, j],
            device_id=(pair, partner), device_id_type=MESH)

    def to_chip(q, way, hops):
        sign = 1 if way == 0 else -1
        ref = block(q, z - sign * hops, core)
        return pltpu.make_async_remote_copy(
            src_ref=ref, dst_ref=ref, send_sem=zs.at[q, way, hops], recv_sem=zr.at[q, way, hops],
            device_id=chip_at(z + sign), device_id_type=MESH)

    def from_chip(q, way, hops):
        sign = 1 if way == 0 else -1
        ref = block(q, z - sign * hops, core)
        return pltpu.make_async_remote_copy(
            src_ref=ref, dst_ref=ref, send_sem=zs.at[q, way, hops - 1], recv_sem=zr.at[q, way, hops - 1],
            device_id=chip_at(z - sign), device_id_type=MESH)

    def to_twin(q, chip):
        ref = block(q, chip, core)
        return pltpu.make_async_remote_copy(
            src_ref=ref, dst_ref=ref, send_sem=cs.at[q, chip], recv_sem=cr.at[q, chip],
            device_id=twin, device_id_type=MESH)

    def from_twin(q, chip):
        ref = block(q, chip, 1 - core)
        return pltpu.make_async_remote_copy(
            src_ref=ref, dst_ref=ref, send_sem=cs.at[q, chip], recv_sem=cr.at[q, chip],
            device_id=twin, device_id_type=MESH)

    def can_send(way, hops):
        if way == 0:
            return (z - hops >= 0) & (z < chips - 1)
        return (z + hops < chips) & (z > 0)

    def can_get(way, hops):
        return z - hops >= 0 if way == 0 else z + hops < chips

    def columns(unit):
        return slice((unit % 2) * half, (unit % 2 + 1) * half)

    for j in range(swaps):
        slot = jnp.clip(live + (j - swaps) // 2, 0, slots - 1)
        v_out[j] = v_ref[slot, :, columns(j - swaps)]
        swap_v(j).start()
    for j in range(swaps):
        slot = jnp.clip(live + (j - swaps) // 2, 0, slots - 1)
        a_out[j] = a_ref[slot, :, columns(j - swaps)]
        swap_a(j).start()

    def stage(q):
        own_unit = min(q, 2 * slots - 1)
        own = v_ref[own_unit // 2, :, columns(own_unit)]
        j = q - (queue - swaps)
        if j >= 0:
            swap_v(j).wait_recv()
            own = jnp.where(q >= queue - taken, v_in[j], own)
        start = pl.multiple_of(pair * rows, 8)
        rows_all[q, pl.ds(start, rows), :] = own
        for way in range(2):
            @pl.when(can_send(way, 0))
            def _():
                to_chip(q, way, 0).start()
        to_twin(q, z).start()

    def relay(q):
        for hops in range(1, chips):
            for way in range(2):
                @pl.when(can_get(way, hops))
                def _():
                    from_chip(q, way, hops).wait_recv()
                    if hops < chips - 1:
                        @pl.when(can_send(way, hops))
                        def _():
                            to_chip(q, way, hops).start()
                    to_twin(q, z - hops if way == 0 else z + hops).start()

    def multiply(q):
        for chip in range(chips):
            from_twin(q, chip).wait_recv()
        own_unit = min(q, 2 * slots - 1)
        j = q - (queue - swaps)
        if j >= 0:
            swap_a(j).wait_recv()
        keep_own = q < keep
        base = (own_unit % 2) * half

        @pl.loop(0, half // DEPTH)
        def _(step):
            inner = pl.ds(pl.multiple_of(step * DEPTH, DEPTH), DEPTH)
            outer = pl.ds(pl.multiple_of(base + step * DEPTH, DEPTH), DEPTH)
            a = jnp.where(keep_own, a_ref[own_unit // 2, :, outer], 0.0)
            if j >= 0:
                a = jnp.where(q >= queue - taken, a_in[j, :, inner], a)
            acc[...] += product(a, rows_all[q, :, inner])

    acc[...] = jnp.zeros_like(acc)
    ahead = queue - swaps
    for q in range(ahead):
        stage(q)
    for q in range(queue):
        relay(q)
        if q + ahead < queue:
            stage(q + ahead)
        multiply(q)

    def part(step):
        to = lax.rem(virt + step, n_virt)
        ref = acc.at[pl.ds(pl.multiple_of(to * out_rows, 8), out_rows), :]
        return pltpu.make_async_remote_copy(
            src_ref=ref, dst_ref=parts.at[step - 1], send_sem=rs.at[step - 1], recv_sem=rr.at[step - 1],
            device_id=(pair, to), device_id_type=MESH)

    for step in range(1, n_virt):
        part(step).start()
    total = acc[pl.ds(pl.multiple_of(virt * out_rows, 8), out_rows), :]
    for step in range(1, n_virt):
        part(step).wait_recv()
        total = total + parts[step - 1]
    out_ref[...] = total

    for step in range(1, n_virt):
        part(step).wait_send()
    for j in range(swaps):
        swap_a(j).wait_send()
        swap_v(j).wait_send()
    for q in range(queue):
        for hops in range(chips - 1):
            for way in range(2):
                @pl.when(can_send(way, hops))
                def _():
                    to_chip(q, way, hops).wait_send()
        for chip in range(chips):
            to_twin(q, chip).wait_send()


def contract(queue, call_id, chips, n_virt, counts, amplitudes, integrals):
    slots, pairs, width = amplitudes.shape
    rows = integrals.shape[1]
    ab = rows * chips * CORES
    swaps, half = slots - 1, width // 2
    f32 = jnp.float32
    dma = pltpu.SemaphoreType.DMA
    return pl.pallas_call(
        functools.partial(kernel, queue, swaps, chips, n_virt),
        out_shape=jax.ShapeDtypeStruct((pairs // n_virt, ab), f32),
        in_specs=[
            pl.BlockSpec(memory_space=pltpu.SMEM),
            pl.BlockSpec(memory_space=pltpu.VMEM),
            pl.BlockSpec(memory_space=pltpu.VMEM),
        ],
        out_specs=pl.BlockSpec(memory_space=pltpu.VMEM),
        scratch_shapes=[
            pltpu.VMEM((queue, ab, half), f32),
            pltpu.VMEM((swaps, pairs, half), f32),
            pltpu.VMEM((swaps, pairs, half), f32),
            pltpu.VMEM((swaps, rows, half), f32),
            pltpu.VMEM((swaps, rows, half), f32),
            pltpu.VMEM((pairs, ab), f32),
            pltpu.VMEM((n_virt - 1, pairs // n_virt, ab), f32),
            dma((2, swaps)),
            dma((2, swaps)),
            dma((queue, 2, chips - 1)),
            dma((queue, 2, chips - 1)),
            dma((queue, chips)),
            dma((queue, chips)),
            dma((n_virt - 1,)),
            dma((n_virt - 1,)),
        ],
        compiler_params=pltpu.CompilerParams(
            collective_id=call_id, has_side_effects=True, vmem_limit_bytes=58 * 1024 * 1024),
    )(counts, amplitudes, integrals)


def on_device(chips, n_virt, amplitudes, integrals, tile_flags, live_count, pair_occ, occ_energy, ab_energy):
    slots = amplitudes.shape[0]
    virt = lax.axis_index("virt")
    other = jnp.roll(live_count, -(n_virt // 2))
    mine, theirs = live_count[virt], other[virt]
    counts = jnp.stack([mine, jnp.minimum(2 * mine, mine + theirs), jnp.maximum(theirs - mine, 0)]).astype(jnp.int32)
    longest = jnp.max(live_count + other)
    sym_integrals = symmetric(integrals, tile_flags)
    least, most = slots + 1, 2 * slots
    ladder = lax.cond(
        longest <= least,
        functools.partial(contract, least, 1, chips, n_virt),
        functools.partial(contract, most, 2, chips, n_virt),
        counts, amplitudes, sym_integrals)
    occ_range = jnp.arange(occ_energy.shape[0], dtype=jnp.int32)
    first_energy = jnp.sum(
        jnp.where(pair_occ[:, 0:1] == occ_range[None, :], occ_energy[None, :], 0.0), axis=1
    )
    second_energy = jnp.sum(
        jnp.where(pair_occ[:, 1:2] == occ_range[None, :], occ_energy[None, :], 0.0), axis=1
    )
    denominator = ab_energy[None, :] - first_energy[:, None] - second_energy[:, None]
    return (ladder, ladder / denominator)


def solution(mesh):
    return jax.shard_map(
        functools.partial(on_device, mesh.shape["pair"] // CORES, mesh.shape["virt"]),
        mesh=mesh,
        in_specs=(
            P("virt", "pair", None),
            P("virt", "pair", None),
            P("virt"),
            P(),
            P(("pair", "virt"), None),
            P(),
            P(),
        ),
        out_specs=(P(("pair", "virt"), None), P(("pair", "virt"), None)),
        check_vma=False,
    )
```

time: 324 us -> 178 us (0.55)
  waiting for transfers between devices: 264 us -> 0 us
  Pallas kernels: 0 us -> 144 us
  matrix products: 18.3 us -> 0 us
  between operations: 14.1 us -> 4.56 us
    all_gather x1 -> x0, waiting for transfers between devices: 222 us -> none  [contract(): piece_rows = lax.all_gather(int_stack, 'pair', axis=1, tiled=True)]
    pallas_call x0 -> x1, Pallas kernels: none -> 144 us  [contract(): pl.pallas_call(functools.partial(kernel, queue, swaps, chips, n_virt), ou...]
    reduce_scatter x1 -> x0, waiting for transfers between devices: 41.8 us -> none  [on_device(): lax.psum_scatter(partial_value, 'virt', scatter_dimension=0, tiled=True)]
    dot_general x2 -> x0, matrix products: 18.3 us -> none  [tile_product(): lax.dot_general(amp_tile, int_rows, (((1,), (1,)), ((), ())), precision=l...]
  transfers between devices with their start and end apart: 2 -> 0, of which waited for: 2 -> 0; matrix products, arithmetic and copies ran while one was open for 0% -> 0% of each run, Pallas kernels for 0% -> 0%
where the time goes in v1:
time: 178 us; the launch traced here: 177 us
  Pallas kernels  144 us (81%)
  local copies, waits for them, and re-layouts  21.9 us (12%)
  other arithmetic  6.47 us (4%)
  between operations  4.56 us (3%)
    pallas_call x1, Pallas kernels, contract(): pl.pallas_call(functools.partial(kernel, queue, swaps, chips, n_virt), ou...  144 us
    reshape x2, local copies, waits for them, and re-layouts, symmetric(): integrals.reshape(integrals.shape[0], integrals.shape[1], TILE, TILE)  12.6 us
    reshape x1, local copies, waits for them, and re-layouts, symmetric(): swapped = jnp.swapaxes(shaped, 2, 3).reshape(integrals.shape)  5.92 us

profile of v1, /device:TPU:0, one launch (start us, length us, event | category | flops | bytes accessed | tf_op | source)
XLA Modules:
  0.0 177.3 jit_solution(7786389797975861678)
XLA Ops:
  0.6 0.8 fusion
  1.4 1.4 add_reduce_fusion
  3.5 0.6 dynamic_slice.7
  4.0 1.3 dynamic_slice.6
  8.5 0.7 pad_add_fusion.1
  9.2 6.1 %reshape.24 = f32[4,48,64,64]{3,2,1,0:T(8,128)} reshape(f32[4,48,4096]{2,1,0:T(8,128)} %param.10) | data formatting | bytes 6291456 | tf_op jit(solution)/shard_map/reshape | solution.py:17
  15.3 6.6 %copy.10 = f32[4,48,64,64]{2,3,1,0:T(8,128)} copy(f32[4,48,64,64]{3,2,1,0:T(8,128)} %reshape.24) | data formatting | bytes 6291456 | tf_op jit(solution)/shard_map/reshape | solution.py:17
  21.9 0.0 copy-start.3
  21.9 5.9 %reshape.25 = f32[4,48,4096]{2,1,0:T(8,128)} reshape(f32[4,48,64,64]{3,2,1,0:T(8,128)} %bitcast.7) | data formatting | bytes 6291456 | tf_op jit(solution)/shard_map/reshape | solution.py:18
  27.8 0.0 copy-done.3
  27.8 3.5 %multiply_add_fusion = f32[4,48,4096]{2,1,0:T(8,128)S(1)} fusion(f32[4,48,4096]{2,1,0:T(8,128)} %param.10, f32[4,48,4096]{2,1,0:T(8,128)} %reshape.25, f32[4]{0:T(128)S(1)} %convert_element_type.7), kind=kLoop, calls=%fused_computation | loop fusion | flops 1572864 | bytes 9437200 | tf_op jit(solution)/shard_map/add | solution.py:19
  31.3 0.0 copy-start.2
  31.3 0.0 copy-start.1
  31.3 0.0 copy-start
  31.3 144.4 %conditional.1 = (f32[32,384]{1,0:T(8,128)S(1)}) conditional(s32[]{:T(128)} %convert_element_type.6, (s32[3]{0:T(128)S(1)}, f32[4,128,4096]{2,1,0:T(8,128)}, f32[4,48,4096]{2,1,0:T(8,128)S(1)}) %tuple.14, (s32[3]{0:T(128)S(1)}, f32[4,128,4096]{2,1,0:T(8,128)}, f32[4,48,4096]{2,1,0:T(8,128)S(1)}) %tuple.14), branch_computations={%region_1.2_spmd, %region_2.3_spmd} | conditional | bytes 8 | solution.py:263
  31.4 144.3 %branch_1_fun.1 = f32[32,384]{1,0:T(8,128)S(1)} custom-call(s32[3]{0:T(128)S(1)} %get-tuple-element.18.counts, f32[4,128,4096]{2,1,0:T(8,128)} %get-tuple-element.19.a_ref, f32[4,48,4096]{2,1,0:T(8,128)S(1)} %get-tuple-element.20.v_ref), custom_call_target="tpu_custom_call" | custom-call | tf_op jit(solution)/shard_map/cond/branch_1_fun/pallas_call | solution.py:223
  175.7 0.0 copy-done.2
  175.7 0.0 copy-done.1
  175.8 0.2 select_reduce_fusion.1
  175.9 0.0 copy-done
  175.9 0.7 subtract_divide_fusion
  176.7 0.6 copy.14
  (2 shorter events, 0.0 us)
Async XLA Ops:
  21.9 5.9 %copy-start.3 = (s32[4]{0:T(128)S(1)}, s32[4]{0:T(128)}, u32[]{:S(2)}) copy-start(s32[4]{0:T(128)} %param.11) | copy-start | bytes 52
  31.3 144.4 %copy-start.2 = (s32[32,2]{0,1:T(2,128)S(1)}, s32[32,2]{0,1:T(2,128)}, u32[]{:S(2)}) copy-start(s32[32,2]{0,1:T(2,128)} %param.13) | copy-start | bytes 772
  31.3 144.4 %copy-start.1 = (f32[200]{0:T(256)S(1)}, f32[200]{0:T(256)}, u32[]{:S(2)}) copy-start(f32[200]{0:T(256)} %param.14) | copy-start | bytes 2404
  31.3 144.6 %copy-start = (f32[384]{0:T(512)S(1)}, f32[384]{0:T(512)}, u32[]{:S(2)}) copy-start(f32[384]{0:T(512)} %param.15) | copy-start | bytes 4612
